TPU v7x, 32 devices: a whole 2x2x4 slice. The times are simulated.
32 devices in a mesh: batch: 8 (over z, y), tensor: 4 (over x, core).
Axes of the slice: x: 2, y: 2, z: 4, core: 2. Of those that a mesh axis runs over, the one named last changes fastest.
Arguments:
- hidden_rows: bfloat16 [16384, 768], P(('batch', 'tensor')), may hold values from -6 to 6
- side_input: bfloat16 [16384, 96], P(('batch', 'tensor')), may hold values from -6 to 6
- segment_ids: int32 [16384], P(('batch', 'tensor')), may hold values from 0 to 2047, as said below
- side_cotangent: bfloat16 [16384, 96], P(('batch', 'tensor')), may hold values from -6 to 6
- backbone_gains: bfloat16 [2, 2, 768], replicated, may hold values from 0.5 to 1.5
- backbone_project: bfloat16 [2, 768, 3, 768], P(None, None, None, 'tensor'), may hold values from -0.21875 to 0.21875
- backbone_mixing: bfloat16 [2, 768, 768], P(None, 'tensor'), may hold values from -0.875 to 0.875
- backbone_expand: bfloat16 [2, 768, 3072], P(None, None, 'tensor'), may hold values from -0.21875 to 0.21875
- backbone_reduce: bfloat16 [2, 3072, 768], P(None, 'tensor'), may hold values from -0.109375 to 0.109375
- side_down: bfloat16 [2, 768, 96], replicated, may hold values from -0.21875 to 0.21875
- side_gate: float32 [2, 96], replicated, may hold values from -2 to 2
- side_gains: bfloat16 [2, 2, 96], replicated, may hold values from 0.25 to 1.75
- side_project: bfloat16 [2, 96, 288], replicated, may hold values from -0.625 to 0.625
- side_mixing: bfloat16 [2, 96, 96], replicated, may hold values from -2.5 to 2.5
- side_expand: bfloat16 [2, 96, 384], replicated, may hold values from -0.625 to 0.625
- side_reduce: bfloat16 [2, 384, 96], replicated, may hold values from -0.3125 to 0.3125
Outputs:
- backbone_out: bfloat16 [16384, 768], P(('batch', 'tensor'))
- side_out: float32 [16384, 96], P(('batch', 'tensor'))
- side_input_grad: float32 [16384, 96], P(('batch', 'tensor'))
- down_grad: float32 [2, 768, 96], replicated
- gate_grad: float32 [2, 96], replicated
- gains_grad: float32 [2, 2, 96], replicated
- project_grad: float32 [2, 96, 288], replicated
- mixing_grad: float32 [2, 96, 96], replicated
- expand_grad: float32 [2, 96, 384], replicated
- reduce_grad: float32 [2, 384, 96], replicated
Inputs may be any that keep to these rules, and one draw needn't show every extreme that they name: `segment_ids`: within each packed sequence of 2048 consecutive rows the ids start at 0, never fall and may skip values; the last row of every sequence has id 2048 - 1; in every sequence one example starts within the first 512 rows and ends within the last 512 rows.
All inputs are finite; a program needn't handle non-finite values.
Results may differ from a plain program's by a relative error of at most 0.033.
Values may be sent and summed in bfloat16 or wider, within the bound.
A program may use at most 128 MiB of HBM per device.

v0:
```python
import functools
import jax
import jax.numpy as jnp
from jax import lax
from jax.experimental import pallas as pl
from jax.experimental.pallas import tpu as pltpu
from jax.sharding import PartitionSpec as P

HEAD_DIM = 64
SIDE_HEADS = 12
SIDE_HEAD_DIM = 8
LAYERS = 2
EPS = 1e-06
BIG = 2.0**100
LOG2E = 1.4426950408889634
ID_BITS = 11
QUAD = 4
MESH = pl.DeviceIdType.MESH
F32 = jnp.float32
BF16 = jnp.bfloat16


def contract(left, right, dims):
    return lax.dot_general(left, right, ((dims[:1], dims[1:]), ((), ())), preferred_element_type=F32)


def nn(left, right):
    return contract(left, right, (1, 0))


def nt(left, right):
    return contract(left, right, (1, 1))


def tn(left, right):
    return contract(left, right, (0, 0))


def lanes_of(rows, lanes):
    return lax.broadcasted_iota(jnp.int32, (rows, lanes), 1)


def segment_lanes(id_row, offset):
    width = id_row.shape[1]
    place = lax.broadcasted_iota(jnp.int32, (128, width), 0) - offset
    flipped = place >= ID_BITS
    shift = jnp.clip(jnp.where(flipped, place - ID_BITS, place), 0, ID_BITS)
    bit = lax.shift_right_logical(jnp.broadcast_to(id_row, (128, width)), shift) & 1
    bit = jnp.where(flipped, 1 - bit, bit)
    used = (place >= 0) & (place < 2 * ID_BITS)
    keys = jnp.where(used, bit, 0).astype(F32)
    queries = jnp.where(used, (bit - 1).astype(F32) * BIG, 0.0)
    return keys.T, queries.T


def root_norm(values, gain):
    return values * lax.rsqrt(jnp.mean(values * values, axis=-1, keepdims=True) + EPS) * gain


class Refs:
    def __init__(self, **refs):
        self.__dict__.update(refs)


def remote(src, dst, send, recv, target):
    return pltpu.make_async_remote_copy(
        src_ref=src, dst_ref=dst, send_sem=send, recv_sem=recv, device_id=target, device_id_type=MESH
    )


class Weights:
    def __init__(self, layer, b, t, c):
        self.layer, self.b, self.t, self.c = layer, b, t, c
        self.part = lax.rem(b, QUAD)
        self.fulls = (c.mix_w, c.exp_w, c.red_w)
        self.sources = (c.mix_hbm, c.exp_hbm, c.red_hbm)
        self.slices = tuple(w.shape[2] // QUAD for w in self.fulls)
        mix, up, down = self.slices
        self.pieces = (
            (0, 0, mix),
            (1, 0, up // 2),
            (1, up // 2, up // 2),
            (2, 0, down // 2),
            (2, down // 2, down // 2),
        )

    def rows(self, p, part):
        w, low, size = self.pieces[p]
        return pl.ds(pl.multiple_of(part * self.slices[w] + low, 16), size)

    def view(self, p, slot, part):
        return self.fulls[self.pieces[p][0]].at[self.layer, slot, self.rows(p, part)]

    def load(self, w):
        return pltpu.make_async_copy(
            self.sources[w].at[self.layer],
            self.fulls[w].at[self.layer, self.t],
            self.c.load_sem.at[self.layer, w],
        )

    def own(self, w, slot):
        c = self.c
        return remote(
            self.sources[w].at[self.layer],
            self.fulls[w].at[self.layer, slot],
            c.own_send.at[self.layer, w],
            c.own_recv.at[self.layer, w],
            (self.b, self.t ^ 1),
        )

    def cross(self, p):
        c = self.c
        return remote(
            self.sources[self.pieces[p][0]].at[self.layer, self.rows(p, self.part)],
            self.view(p, self.t, self.part),
            c.cross_send.at[self.layer, p],
            c.w_recv.at[self.layer, p, self.part],
            (self.b, self.t ^ 2),
        )

    def spread(self, p, k):
        c = self.c
        view = self.view(p, self.t ^ 2, self.part)
        return remote(
            view, view, c.spread_send.at[self.layer, p, k - 1], c.w_recv.at[self.layer, p, self.part], (self.b ^ k, self.t)
        )

    def here(self, p, k):
        c = self.c
        view = self.view(p, self.t ^ 2, self.part ^ k)
        return remote(
            view, view, c.cross_send.at[self.layer, p], c.w_recv.at[self.layer, p, self.part ^ k], (self.b, self.t ^ 2)
        )

    def forward(self, p, k, slot):
        c = self.c
        view = self.view(p, slot, self.part ^ k)
        return remote(
            view,
            view,
            c.pass_send.at[self.layer, p, k],
            c.pass_recv.at[self.layer, p, self.part ^ k],
            (self.b, self.t ^ 1),
        )

    def start_cross(self):
        for p in range(5):
            self.cross(p).start()

    def start_spread(self, p):
        self.here(p, 0).wait_recv()
        for k in range(1, QUAD):
            self.spread(p, k).start()

    def start_forward(self, p):
        for k in range(1, QUAD):
            self.here(p, k).wait_recv()
        for k in range(QUAD):
            self.forward(p, k, self.t ^ 2).start()

    def wait_far(self, p):
        for k in range(QUAD):
            self.forward(p, k, self.t ^ 3).wait_recv()

    def wait_sent(self):
        for w in range(3):
            self.own(w, self.t).wait_send()
        for p in range(5):
            self.cross(p).wait_send()
            for k in range(1, QUAD):
                self.spread(p, k).wait_send()
            for k in range(QUAD):
                self.forward(p, k, self.t ^ 2).wait_send()


class Backbone:
    def __init__(self, layer, b, t, parts, c):
        self.layer, self.b, self.t, self.parts, self.c = layer, b, t, parts, c
        self.sib, self.across, self.far = t ^ 1, t ^ 2, t ^ 3
        self.tokens = c.rows_all.shape[1]
        self.half = self.tokens // 2
        self.width = c.mix_w.shape[2]
        self.heads = self.width // HEAD_DIM
        self.weights = Weights(layer, b, t, c)

    def row_copy(self, slot, chunk, send, target):
        c = self.c
        view = c.rows_all.at[slot, pl.ds(chunk * self.half, self.half)]
        return remote(
            view,
            view,
            c.row_send.at[self.layer, send, chunk],
            c.row_recv.at[self.layer, slot, chunk],
            (self.b, target),
        )

    def norm_rows(self, stream):
        c = self.c
        gain = c.gains[self.layer, 0:1, :].astype(F32)
        c.rows_all[self.t] = root_norm(stream, gain).astype(BF16)

    def send_rows(self):
        for chunk in range(2):
            self.row_copy(self.t, chunk, 1, self.across).start()
        for chunk in range(2):
            self.row_copy(self.t, chunk, 0, self.sib).start()

    def project(self, slot, chunk):
        c, width, half = self.c, self.width, self.half
        inside = pl.ds(pl.multiple_of(chunk * half, half), half)
        rows = c.rows_all[slot, inside, :]
        at = pl.ds(pl.multiple_of(slot * self.tokens + chunk * half, half), half)
        lane = lanes_of(half, 128)
        query = nt(rows, c.qkv_w[self.layer, 0]) * (HEAD_DIM**-0.5 * LOG2E)
        keys = nt(rows, c.qkv_w[self.layer, 1])
        bits = segment_lanes(c.ids_all[slot, 0:1, inside], HEAD_DIM)
        for target, columns, high in ((c.k_s, keys, bits[0]), (c.q_s, query, bits[1])):
            low = pltpu.roll(high, HEAD_DIM, 1)
            for h in range(self.heads):
                own = columns[:, h // 2 * 128 : h // 2 * 128 + 128]
                inner = jnp.where(lane < HEAD_DIM, own, high) if h % 2 == 0 else jnp.where(lane < HEAD_DIM, low, own)
                target[h, at] = inner.astype(BF16)
        values = nt(c.qkv_w[self.layer, 2, 0:width], rows)
        for h in range(self.heads):
            c.vt_s[h, 0:HEAD_DIM, at] = values[h * HEAD_DIM : (h + 1) * HEAD_DIM].astype(BF16)
            c.vt_s[h, HEAD_DIM:, at] = jnp.ones((16, half), BF16)

    def project_all(self, first, last, hook):
        def step(index, carry):
            for chunk in range(2):

                @pl.when(index == 2 + chunk)
                def _():
                    self.row_copy(self.sib, chunk, 0, self.sib).wait_recv()

                @pl.when(index == 4 + 2 * chunk)
                def _():
                    self.row_copy(self.across, chunk, 0, self.sib).wait_recv()
                    self.row_copy(self.across, chunk, 2, self.sib).start()

                @pl.when(index == 5 + 2 * chunk)
                def _():
                    self.row_copy(self.far, chunk, 0, self.sib).wait_recv()

            hook(index)
            early = index < 4
            k = jnp.where(early, index // 2, 2 + index % 2)
            chunk = jnp.where(early, index % 2, index // 2 - 2)
            self.project(self.t ^ k, chunk)
            return carry

        lax.fori_loop(first, last, step, 0)

    def wait_rows(self):
        for chunk in range(2):
            self.row_copy(self.t, chunk, 0, self.sib).wait_send()
            self.row_copy(self.t, chunk, 1, self.across).wait_send()
            self.row_copy(self.across, chunk, 2, self.sib).wait_send()

    def block_of(self, item):
        return self.t ^ (self.parts - 1 - item // self.heads)

    def make_scores(self, item, place):
        c = self.c
        h = lax.rem(item, self.heads)
        at = pl.ds(pl.multiple_of(self.block_of(item) * self.tokens, self.tokens), self.tokens)
        c.scores[place] = nt(c.k_s[h], c.q_s[h, at])

    def send_heads(self, block):
        c = self.c
        return remote(
            c.heads_buf.at[block],
            c.heads_buf.at[self.parts + self.t],
            c.head_send.at[self.layer, block],
            c.head_recv.at[self.layer, self.t],
            (self.b, block),
        )

    def attend(self, item, place):
        c = self.c
        block = self.block_of(item)
        h = lax.rem(item, self.heads)
        values = c.scores[place]
        weights = jnp.exp2(values - jnp.max(values, axis=0, keepdims=True)).astype(BF16)
        out = nn(c.vt_s[h], weights)
        slot = jnp.where(block == self.t, self.parts + self.t, block)
        c.heads_buf[slot, pl.ds(pl.multiple_of(h * HEAD_DIM, HEAD_DIM), HEAD_DIM), :] = (
            out[0:HEAD_DIM] * (1.0 / out[HEAD_DIM : HEAD_DIM + 1])
        ).astype(BF16)

        @pl.when((h == self.heads - 1) & (item < (self.parts - 1) * self.heads))
        def _():
            self.send_heads(block).start()

    def attention(self, hook):
        count = self.parts * self.heads
        self.make_scores(0, 0)

        def pair(index, carry):
            item = 2 * index
            hook(index)
            self.make_scores(item + 1, 1)
            self.attend(item, 0)
            self.make_scores(jnp.minimum(item + 2, count - 1), 0)
            self.attend(item + 1, 1)
            return carry

        lax.fori_loop(0, count // 2, pair, 0)

    def wait_heads(self):
        c = self.c
        for k in range(1, self.parts):
            self.send_heads(self.t ^ k).wait_send()
            remote(
                c.heads_buf.at[0],
                c.heads_buf.at[self.parts + (self.t ^ k)],
                c.head_send.at[self.layer, 0],
                c.head_recv.at[self.layer, self.t ^ k],
                (self.b, self.sib),
            ).wait_recv()

    def feed_forward(self, stream, hook):
        c, parts, layer = self.c, self.parts, self.layer
        attended = c.heads_buf[parts : 2 * parts].reshape(parts * self.width, self.tokens)
        stream = stream + tn(attended, c.mix_w[layer].reshape(parts * self.width, -1))
        c.acc[...] = stream
        c.normed[...] = root_norm(stream, c.gains[layer, 1:2, :].astype(F32)).astype(BF16)

        def feed(index, carry):
            hook(index)
            hidden = jax.nn.gelu(nn(c.normed[...], c.exp_w[layer, self.t ^ index])).astype(BF16)
            c.acc[...] += nn(hidden, c.red_w[layer, self.t ^ index])
            return carry

        lax.fori_loop(0, parts, feed, 0)


FRONT_SCRATCH = (
    *("vectors", "rows_all", "ids_scratch", "qkv_w", "mix_w", "exp_w", "red_w", "q_s", "k_s", "vt_s", "scores"),
    *("heads_buf", "acc", "normed", "load_sem", "qkv_sem", "row_send", "row_recv", "id_send", "id_recv"),
    *("head_send", "head_recv", "cross_send", "spread_send", "pass_send", "own_send", "w_recv", "pass_recv"),
    *("own_recv", "side_k", "side_vt", "kv_send", "kv_recv"),
)


def front_kernel(parts, *refs):
    refs = list(refs)

    def pop(count):
        taken, refs[:count] = refs[:count], []
        return taken

    x_ref, ids_ref, gains, qkv_hbm, mix_hbm, exp_hbm, red_hbm, side_in = pop(8)
    raw = Refs(**dict(zip(RAW, pop(7))))
    second_f, *handed = pop(11)
    local = pop(10)
    first_f, ids_all, state_one, kvt = local[0:4]
    keep = Refs(**dict(zip(KEEP, local[4:])))
    hand_sem = pop(1)[0]
    hand = [pltpu.make_async_copy(*pair, hand_sem.at[k]) for k, pair in enumerate(zip(local, handed))]
    prev = pop(1)[0]
    w = Refs(**dict(zip(WEIGHTS, pop(5))))
    c = Refs(**dict(zip(FRONT_SCRATCH, pop(len(FRONT_SCRATCH)))))
    c.gains, c.mix_hbm, c.exp_hbm, c.red_hbm, c.ids_all = gains, mix_hbm, exp_hbm, red_hbm, ids_all
    b = lax.axis_index("batch")
    t = lax.axis_index("tensor")
    tokens = x_ref.shape[0]
    width = c.mix_w.shape[2]
    lower, upper = Backbone(0, b, t, parts, c), Backbone(1, b, t, parts, c)
    load_qkv = [
        pltpu.make_async_copy(
            qkv_hbm.at[layer, k], c.qkv_w.at[layer, k, pl.ds(0, width)], c.qkv_sem.at[layer, k]
        )
        for layer in range(LAYERS)
        for k in range(3)
    ]
    for copy in load_qkv:
        copy.start()
    for layer in (lower, upper):
        for k in range(3):
            layer.weights.load(k).start()
    barrier = tensor_barrier(b, t, parts)
    for k in range(1, QUAD):
        pl.semaphore_signal(barrier, inc=1, device_id=(b ^ k, t), device_id_type=MESH)
    lower.norm_rows(x_ref[...].astype(F32))
    ids_all[t] = jnp.broadcast_to(ids_ref[...], (8, tokens))
    pl.semaphore_wait(barrier, parts - 1 + QUAD - 1)

    def id_copy(slot, k):
        return remote(ids_all.at[slot], ids_all.at[slot], c.id_send.at[k - 1], c.id_recv.at[slot], (b, t ^ k))

    for k in range(1, parts):
        id_copy(t, k).start()
    lower.weights.cross(1).start()
    lower.send_rows()
    for k in range(3):
        lower.weights.own(k, t).start()
    c.qkv_w[:, :, width:, :] = jnp.zeros((LAYERS, 3, 256 - width, x_ref.shape[1]), BF16)
    for copy in load_qkv:
        copy.wait()
    load_side_weights(0, w, raw)
    load_vectors(c.vectors, raw)
    raw.vectors = c.vectors
    prev[...] = widened(side_in)
    for k in range(1, parts):
        id_copy(t, k).wait_send()
        id_copy(t ^ k, k).wait_recv()

    def when(index, at, act, *args):
        @pl.when(index == at)
        def _():
            act(*args)

    def lower_project(index):
        when(index, 4, lower.weights.start_spread, 1)
        for p in (0, 2, 3, 4):
            when(index, 6, lambda p: lower.weights.cross(p).start(), p)

    def lower_attention(index):
        for at, p in ((1, 0), (2, 2), (3, 3), (5, 4)):
            when(index, at, lower.weights.start_spread, p)
        for at, p in ((4, 1), (5, 0)):
            when(index, at, lower.weights.start_forward, p)

    def feed_hook(layer):
        def hook(index):
            weights = layer.weights

            @pl.when(index == 0)
            def _():
                for k in (1, 2):
                    weights.load(k).wait()
                if layer is lower:
                    weights.start_forward(2)

            @pl.when(index == 1)
            def _():
                for k in (1, 2):
                    weights.own(k, layer.sib).wait_recv()
                if layer is lower:
                    weights.start_forward(3)

            @pl.when(index == 2)
            def _():
                if layer is lower:
                    weights.start_forward(4)

            @pl.when(index == 3)
            def _():
                for p in range(1, 5):
                    weights.wait_far(p)

        return hook

    lower.project_all(0, 2 * parts, lower_project)
    lower.wait_rows()
    lower.attention(lower_attention)
    upper.weights.start_cross()
    for k in range(3):
        upper.weights.own(k, t).start()
    lower.weights.load(0).wait()
    lower.weights.own(0, lower.sib).wait_recv()
    lower.weights.wait_far(0)
    lower.wait_heads()
    lower.feed_forward(x_ref[...].astype(F32), feed_hook(lower))
    first_f[...] = c.acc[...].astype(BF16)

    side = Refs(
        kvt=kvt, k_s=c.side_k, vt_s=c.side_vt, scores=c.scores, kv_send=c.kv_send, kv_recv=c.kv_recv
    )

    def send_upper():
        upper.norm_rows(c.acc[...])
        upper.send_rows()

    def side_hook(index):
        for p in range(5):
            when(index, p, upper.weights.start_spread, p)

    side_forward(
        0, b, t, parts, first_f, prev, w, raw, side, keep, ids_all, state_one,
        send_upper, lambda: upper.project_all(0, parts, lambda index: None), side_hook,
    )

    for copy in hand:
        copy.start()

    def upper_attention(index):
        for p in range(5):
            when(index, p + 1, upper.weights.start_forward, p)

    upper.project_all(parts, 2 * parts, lambda index: None)
    upper.wait_rows()
    upper.attention(upper_attention)
    upper.weights.load(0).wait()
    upper.weights.own(0, upper.sib).wait_recv()
    upper.weights.wait_far(0)
    upper.wait_heads()
    upper.feed_forward(c.acc[...], feed_hook(upper))
    second_f[...] = c.acc[...].astype(BF16)
    for copy in hand:
        copy.wait()
    lower.weights.wait_sent()
    upper.weights.wait_sent()


def front_call(x, ids, gains, qkv, mix, exp, red, side_in, raw, parts):
    tokens, model = x.shape
    width = mix.shape[1]
    units = exp.shape[2]
    heads = width // HEAD_DIM
    length = parts * tokens
    side_units = raw[5].shape[2]
    anywhere = pl.BlockSpec(memory_space=pl.ANY)
    dma = pltpu.SemaphoreType.DMA
    vmem = pltpu.VMEM
    outs = (
        ((tokens, model), BF16),
        ((tokens, model), BF16),
        ((parts, 8, tokens), jnp.int32),
        ((tokens, 128), F32),
        ((parts, 192, tokens), BF16),
        *keep_shapes(tokens),
    )
    return pl.pallas_call(
        functools.partial(front_kernel, parts),
        out_shape=tuple(jax.ShapeDtypeStruct(*o) for o in outs),
        in_specs=vmem_specs(3) + [anywhere] * 4 + vmem_specs(8),
        out_specs=(*vmem_specs(1), *[anywhere] * 10),
        scratch_shapes=[
            *[vmem(*out) for out in outs[1:]],
            dma((10,)),
            vmem((tokens, 128), F32),
            *weight_scratch(model, side_units),
            vmem((LAYERS, 8, 128), F32),
            vmem((parts, tokens, model), BF16),
            vmem((8, 128), F32),
            vmem((LAYERS, 3, 256, model), BF16),
            vmem((LAYERS, parts, width, model), BF16),
            vmem((LAYERS, parts, model, units), BF16),
            vmem((LAYERS, parts, units, model), BF16),
            vmem((heads, length, 128), BF16),
            vmem((heads, length, 128), BF16),
            vmem((heads, HEAD_DIM + 16, length), BF16),
            vmem((2, length, tokens), F32),
            vmem((2 * parts, width, tokens), BF16),
            vmem((tokens, model), F32),
            vmem((tokens, model), BF16),
            dma((LAYERS, 3)),
            dma((LAYERS, 3)),
            dma((LAYERS, 3, 2)),
            dma((LAYERS, parts, 2)),
            dma((parts - 1,)),
            dma((parts,)),
            dma((LAYERS, parts)),
            dma((LAYERS, parts)),
            dma((LAYERS, 5)),
            dma((LAYERS, 5, QUAD - 1)),
            dma((LAYERS, 5, QUAD)),
            dma((LAYERS, 3)),
            dma((LAYERS, 5, QUAD)),
            dma((LAYERS, 5, QUAD)),
            dma((LAYERS, 3)),
            vmem((length, 128), BF16),
            vmem((SIDE_HEADS, 16, length), BF16),
            dma((3,)),
            dma((parts,)),
        ],
        compiler_params=pltpu.CompilerParams(
            collective_id=1, has_side_effects=True, vmem_limit_bytes=62 << 20
        ),
    )(x, ids, gains, qkv, mix, exp, red, side_in, *raw)


LN2 = 0.6931471805599453
COLUMNS = 16
EARLY = (6, 7, 8, 9, 10, 11, 12, 13)
LATE = (0, 1, 2, 3, 4, 5, 14, 15)


def place_of(column):
    order, low = (EARLY, 0) if column in EARLY else (LATE, 2)
    index = order.index(column)
    return index // 2 * 4 + low + index % 2


RING = 8


def side_norm(values, width):
    rstd = lax.rsqrt(jnp.sum(values * values, axis=-1, keepdims=True) * (1.0 / width) + EPS)
    return values * rstd, rstd


def gelu_parts(inner):
    root = 0.7978845608028654
    square = inner * inner
    curve = jnp.tanh(root * inner * (1.0 + 0.044715 * square))
    half = 0.5 * (1.0 + curve)
    slope = half + 0.5 * inner * (1.0 - curve * curve) * root * (1.0 + 3 * 0.044715 * square)
    return inner * half, slope


def load_side_weights(layer, w, raw):
    side = raw.mixing.shape[1]
    w.down[side:, :] = jnp.zeros_like(w.down[side:, :])
    w.down[0:side, :] = raw.down[layer]
    w.project[...] = jnp.zeros_like(w.project)
    w.project[0:side, 0 : 3 * side] = raw.project[layer]
    w.mixing[...] = jnp.zeros_like(w.mixing)
    w.mixing[0:side, 0:side] = raw.mixing[layer]
    w.expand[side:, :] = jnp.zeros_like(w.expand[side:, :])
    w.expand[0:side, :] = raw.expand[layer]
    w.reduce[side:, :] = jnp.zeros_like(w.reduce[side:, :])
    w.reduce[0:side, :] = raw.reduce[layer]


def load_vectors(vectors, raw):
    side = raw.mixing.shape[1]
    vectors[...] = jnp.zeros_like(vectors)
    for layer in range(LAYERS):
        vectors[layer, 0:1, 0:side] = raw.gate[layer : layer + 1, :]
        vectors[layer, 1:3, 0:side] = raw.gains[layer].astype(F32)


def widened(turned):
    values = turned[...].astype(F32)
    return jnp.concatenate([values, jnp.zeros((32, values.shape[1]), F32)], axis=0).T


def kv_copy(c, slot, send, target):
    return remote(c.kvt.at[slot], c.kvt.at[slot], c.kv_send.at[send], c.kv_recv.at[slot], target)


def keys_from(c, slot, ids_ref):
    tokens = c.kvt.shape[2]
    at = pl.ds(pl.multiple_of(slot * tokens, tokens), tokens)
    key_bits, _ = segment_lanes(ids_ref[slot][0:1, :], 96)
    keys = jnp.concatenate([c.kvt[slot, 0:96].astype(F32), jnp.zeros((32, tokens), F32)], axis=0)
    c.k_s[at, 0:128] = (keys.T + key_bits).astype(BF16)


def side_forward(layer, b, t, parts, f_ref, prev, w, raw, c, keep, ids_ref, result, after_send, meanwhile, between):
    side = raw.mixing.shape[1]
    tokens = f_ref.shape[0]
    gate = jax.nn.sigmoid(raw.vectors[layer, 0:1, :])
    lifted = nt(f_ref[...], w.down[...])
    mixed = gate * lifted + (1.0 - gate) * prev[...]
    keep.lifted[...] = lifted
    keep.mixed[...] = mixed
    normed = (side_norm(mixed, side)[0] * raw.vectors[layer, 1:2, :]).astype(BF16)
    turned = w.project[...].astype(F32).T.astype(BF16)
    c.kvt[t] = nt(turned[side : 3 * side], normed).astype(BF16)
    sib, across, far = t ^ 1, t ^ 2, t ^ 3
    kv_copy(c, t, 1, (b, across)).start()
    kv_copy(c, t, 0, (b, sib)).start()
    after_send()
    lane = lanes_of(tokens, 128)
    weight_q = jnp.where(lanes_of(128, 128) < side, w.project[:, 0:128], jnp.zeros((128, 128), BF16))
    query_bits = segment_lanes(ids_ref[t][0:1, :], 96)[1]
    keep.query[...] = (
        nn(normed, weight_q) * (SIDE_HEAD_DIM**-0.5 * LOG2E) + query_bits
    ).astype(BF16)
    keep.sums[...] = jnp.zeros_like(keep.sums)

    def take(index, carry):
        @pl.when(index == 1)
        def _():
            kv_copy(c, sib, 0, (b, sib)).wait_recv()

        @pl.when(index == 2)
        def _():
            meanwhile()
            kv_copy(c, across, 0, (b, sib)).wait_recv()
            kv_copy(c, across, 2, (b, sib)).start()

        @pl.when(index == 3)
        def _():
            kv_copy(c, far, 0, (b, sib)).wait_recv()

        slot = t ^ index
        at = pl.ds(pl.multiple_of(slot * tokens, tokens), tokens)
        keys_from(c, slot, ids_ref)
        values = c.kvt[slot, 96:192].astype(F32)
        for h in range(SIDE_HEADS):
            c.vt_s[h, :, at] = jnp.concatenate(
                [values[8 * h : 8 * h + 8], jnp.ones((8, tokens), F32)], axis=0
            ).astype(BF16)
        return carry

    lax.fori_loop(0, parts, take, 0)

    def make_scores(h, place):
        rows = keep.query[...]
        chosen = (lane // SIDE_HEAD_DIM == h) | (lane >= side)
        c.scores[place] = nt(c.k_s[:, 0:128], jnp.where(chosen, rows, jnp.zeros_like(rows)))

    def attend(h, place):
        values = c.scores[place]
        top = jnp.max(values, axis=0, keepdims=True)
        out = nn(c.vt_s[h], jnp.exp2(values - top).astype(BF16))
        total = out[8:9]
        keep.heads[pl.ds(pl.multiple_of(h * 8, 8), 8), :] = out[0:8] * (1.0 / total)
        here = lax.broadcasted_iota(jnp.int32, keep.sums.shape, 0) == h
        keep.sums[...] = jnp.where(here, top + jnp.log2(total), keep.sums[...])

    make_scores(0, 0)

    def pair(index, carry):
        h = 2 * index
        between(index)
        make_scores(h + 1, 1)
        attend(h, 0)
        make_scores(jnp.minimum(h + 2, SIDE_HEADS - 1), 0)
        attend(h + 1, 1)
        return carry

    lax.fori_loop(0, SIDE_HEADS // 2, pair, 0)
    kv_copy(c, t, 1, (b, across)).wait_send()
    kv_copy(c, t, 0, (b, sib)).wait_send()
    kv_copy(c, across, 2, (b, sib)).wait_send()
    middle = mixed + tn(keep.heads[...].astype(BF16), w.mixing[0:side, :])
    keep.middle[...] = middle
    normed_two = (side_norm(middle, side)[0] * raw.vectors[layer, 2:3, :]).astype(BF16)
    active = jax.nn.gelu(nn(normed_two, w.expand[...])).astype(BF16)
    result[...] = middle + nt(active, w.reduce[...])


def norm_back(values, gain, grad, side):
    hat, rstd = side_norm(values, side)
    gain_grad = jnp.sum(grad * hat, axis=0, keepdims=True)
    pulled = grad * gain
    mean = jnp.sum(pulled * hat, axis=-1, keepdims=True) * (1.0 / side)
    return rstd * (pulled - hat * mean), gain_grad


def pad_heads(target, rows, fill):
    for h in range(SIDE_HEADS):
        target[h] = jnp.concatenate(
            [rows[8 * h : 8 * h + 8], jnp.full((8, rows.shape[1]), fill, F32)], axis=0
        ).astype(BF16)


def side_prepare(layer, parts, w, raw, c, keep, kvt, ids_ref, again):
    side = raw.mixing.shape[1]
    tokens = c.q_s.shape[1]
    lane = lanes_of(tokens, 128)
    normed_two = side_norm(keep.middle[...], side)[0] * raw.vectors[layer, 2:3, :]
    active, slope = gelu_parts(nn(normed_two.astype(BF16), w.expand[...]))
    c.active[layer] = active.astype(BF16)
    c.slope[layer] = slope
    sums = keep.sums[...]
    rows = jnp.concatenate([sums, sums, sums, jnp.zeros((80, tokens), F32)], axis=0).T
    high = rows.astype(BF16).astype(F32)
    mid = (rows - high).astype(BF16).astype(F32)
    low = rows - high - mid
    rows = jnp.where(lane < 16, high, jnp.where(lane < 32, mid, low))
    query = keep.query[...]
    c.q_s[layer, :, 0:128] = query
    c.q_s[layer, :, 128:256] = jnp.where(lane < 48, -rows, 0.0).astype(BF16)
    pad_heads(c.qt_s.at[layer], query.astype(F32).T, 0.0)

    def take(slot, carry):
        at = pl.ds(pl.multiple_of(slot * tokens, tokens), tokens)
        if again:
            keys_from(Refs(kvt=kvt, k_s=c.k_s.at[layer]), slot, ids_ref)
        c.k_s[layer, at, 128:256] = jnp.where(lane < 48, 1.0, 0.0).astype(BF16)
        values = jnp.concatenate([kvt[slot, 96:192].astype(F32), jnp.ones((32, tokens), F32)], axis=0)
        c.v_s[layer, at, :] = values.T.astype(BF16)
        keys = kvt[slot, 0:96].astype(F32)
        for h in range(SIDE_HEADS):
            c.kt_s[layer, h, :, at] = jnp.concatenate(
                [keys[8 * h : 8 * h + 8], jnp.zeros((8, tokens), F32)], axis=0
            ).astype(BF16)
        return carry

    lax.fori_loop(0, parts, take, 0)


def side_backward(layer, b, t, parts, f_ref, prev, w, raw, c, keep, grad_ref, pack, between, early):
    side = raw.mixing.shape[1]
    tokens = f_ref.shape[0]
    gate = jax.nn.sigmoid(raw.vectors[layer, 0:1, :])
    lane = lanes_of(tokens, 128)
    grad = grad_ref[...]
    middle = keep.middle[...]
    gain_two = raw.vectors[layer, 2:3, :]
    normed_two = (side_norm(middle, side)[0] * gain_two).astype(BF16)
    top = grad.astype(BF16)
    reduce_grad = tn(top, c.active[layer])
    grad_inner = (c.slope[layer] * nn(top, w.reduce[...])).astype(BF16)
    expand_grad = tn(normed_two, grad_inner)
    for k in range(3):
        pack[place_of(6 + k)] = expand_grad[0:96, 128 * k : 128 * k + 128]
        pack[place_of(9 + k)] = reduce_grad[0:96, 128 * k : 128 * k + 128]
    through, gain_two_grad = norm_back(middle, gain_two, nt(grad_inner, w.expand[...]), side)
    grad_middle = grad + through
    branch = grad_middle.astype(BF16)
    heads = keep.heads[...]
    mixing_grad = nn(heads.astype(BF16), branch)
    grad_heads = nt(branch, w.mixing[...]).astype(BF16).astype(F32).T
    product = grad_heads[0:96] * heads
    group = lax.broadcasted_iota(jnp.int32, (16, 96), 1) // SIDE_HEAD_DIM
    group = (group == lax.broadcasted_iota(jnp.int32, (16, 96), 0)).astype(BF16)
    high = product.astype(BF16)
    inner = nn(group, high) + nn(group, (product - high.astype(F32)).astype(BF16))
    rows = jnp.concatenate([grad_heads[0:96], -inner, -inner], axis=0).T
    high = rows.astype(BF16)
    c.do_s[...] = jnp.where(lane < 112, high, (rows - high.astype(F32)).astype(BF16))
    pad_heads(c.dot_s, grad_heads, 0.0)
    wide = lanes_of(tokens, 256)
    query_head = jnp.where(wide < 96, wide // SIDE_HEAD_DIM, jnp.where(wide < 128, -1, (wide - 128) % 16))
    out_head = jnp.where(lane < 96, lane // SIDE_HEAD_DIM, (lane - 96) % 16)

    count = parts * tokens // 2

    def one_head(h, keys):
        rows = c.q_s[layer]
        rows = jnp.where((query_head == h) | (query_head < 0), rows, jnp.zeros_like(rows))
        probs = jnp.exp2(nt(rows, c.k_s[layer, keys, :]))
        rows = c.do_s[...]
        rows = jnp.where(out_head == h, rows, jnp.zeros_like(rows))
        scores = (probs * nt(rows, c.v_s[layer, keys, :])).astype(BF16)
        by_keys = nn(c.qt_s[layer, h], scores)[0:8] * LN2
        by_values = nn(c.dot_s[h], probs.astype(BF16))[0:8]
        return by_keys, by_values, nt(c.kt_s[layer, h, :, keys], scores)[0:8] * SIDE_HEAD_DIM**-0.5

    def terms_copy(pair, k):
        return remote(
            c.terms.at[pair, t ^ k],
            c.terms_in.at[layer, pair, t],
            c.terms_send.at[layer, pair, k - 1],
            c.terms_recv.at[layer, pair, t],
            (b, t ^ k),
        )

    def terms_wait(pair, k):
        return remote(
            c.terms.at[pair, t ^ k],
            c.terms_in.at[layer, pair, t ^ k],
            c.terms_send.at[layer, pair, k - 1],
            c.terms_recv.at[layer, pair, t ^ k],
            (b, t ^ k),
        )

    def pair_of(index, carry):
        between(index)
        queries = jnp.zeros((16, tokens), F32)
        for near in range(2):
            chip = t // 2 if near else (t // 2) ^ 1
            keys = pl.ds(pl.multiple_of(chip * count, count), count)
            first, second = one_head(2 * index, keys), one_head(2 * index + 1, keys)
            by_keys, by_values, by_queries = (
                jnp.concatenate([left, right], axis=0) for left, right in zip(first, second)
            )
            queries += by_queries
            for place in range(parts // 2):
                at = slice(place * tokens, (place + 1) * tokens)
                c.terms[index, chip * (parts // 2) + place, 0:16] = by_keys[:, at].astype(BF16)
                c.terms[index, chip * (parts // 2) + place, 16:32] = by_values[:, at].astype(BF16)
            for k in (1,) if near else (2, 3):
                terms_copy(index, k).start()
        c.dqkv[pl.ds(pl.multiple_of(index * 16, 16), 16), :] = queries.astype(BF16)
        return carry

    pairs = SIDE_HEADS // 2
    lax.fori_loop(0, pairs, pair_of, 0)
    mixed = keep.mixed[...]
    gain_one = raw.vectors[layer, 1:2, :]
    normed = side_norm(mixed, side)[0] * gain_one
    c.dqkv[288:384, :] = jnp.zeros((96, tokens), BF16)

    def gather(index, carry):
        total = c.terms[index, t].astype(F32)
        for k in range(1, parts):
            terms_wait(index, k).wait_recv()
            total += c.terms_in[layer, index, t ^ k].astype(F32)
        total = total.astype(BF16)
        c.dqkv[pl.ds(pl.multiple_of(96 + index * 16, 16), 16), :] = total[0:16]
        c.dqkv[pl.ds(pl.multiple_of(192 + index * 16, 16), 16), :] = total[16:32]
        return carry

    lax.fori_loop(0, pairs, gather, 0)
    dqkv = c.dqkv[...]
    project_grad = nt(normed.T.astype(BF16), dqkv)
    pack[place_of(12)] = project_grad[0:96, 0:128]
    pack[place_of(13)] = project_grad[0:96, 128:256]
    pack[place_of(14)] = project_grad[0:96, 256:384] + pltpu.roll(mixing_grad, 32, 1)
    early()
    grad_normed = nn(w.project[...], dqkv).T
    through, gain_one_grad = norm_back(mixed, gain_one, grad_normed, side)
    grad_mixed = grad_middle + through
    down_grad = nn((gate * grad_mixed).T.astype(BF16), f_ref[...])
    for k in range(6):
        pack[place_of(k)] = down_grad[0:96, 128 * k : 128 * k + 128]
    gate_grad = jnp.sum(grad_mixed * (keep.lifted[...] - prev[...]), axis=0, keepdims=True)
    gate_grad = gate_grad * gate * (1.0 - gate)
    row = lax.broadcasted_iota(jnp.int32, (96, 128), 0)
    pack[place_of(15)] = jnp.where(
        row == 0, gate_grad, jnp.where(row == 1, gain_one_grad, jnp.where(row == 2, gain_two_grad, 0.0))
    )
    grad_ref[...] = (1.0 - gate) * grad_mixed

    def sent(index, carry):
        for k in range(1, parts):
            terms_copy(index, k).wait_send()
        return carry

    lax.fori_loop(0, pairs, sent, 0)


class Sum:
    def __init__(self, r, b, t, parts, batch, pack, s):
        self.r, self.b, self.t, self.parts, self.batch, self.pack, self.s = r, b, t, parts, batch, pack, s
        self.place = lax.rem(b, RING)
        self.outer = batch // RING

    def across_tensor(self, half, k):
        r, s, t = self.r, self.s, self.t
        group = COLUMNS // self.parts
        return remote(
            s.out.at[r, pl.ds((t ^ k) * group + half * (group // 2), group // 2)],
            s.one.at[r, t, pl.ds(half * (group // 2), group // 2)],
            s.one_send.at[r, half, k - 1],
            s.one_recv.at[r, half, t],
            (self.b, t ^ k),
        )

    def from_tensor(self, half, k):
        r, s, t = self.r, self.s, self.t
        group = COLUMNS // self.parts
        view = s.one.at[r, t ^ k, pl.ds(half * (group // 2), group // 2)]
        return remote(view, view, s.one_send.at[r, half, k - 1], s.one_recv.at[r, half, t ^ k], (self.b, t ^ k))

    def across_batch(self, k):
        r, s = self.r, self.s
        return remote(
            s.mid_out.at[r, self.place ^ k], s.two.at[r, self.place], s.two_send.at[r, k - 1],
            s.two_recv.at[r, self.place], (self.b ^ k, self.t),
        )

    def from_batch(self, k):
        r, s = self.r, self.s
        return remote(
            s.two.at[r, self.place ^ k], s.two.at[r, self.place ^ k], s.two_send.at[r, k - 1],
            s.two_recv.at[r, self.place ^ k], (self.b ^ k, self.t),
        )

    def across_outer(self, k):
        r, s = self.r, self.s
        mine = self.b // RING
        target = lax.rem(mine + k, self.outer) * RING + self.place
        return remote(
            s.far.at[r, mine], s.far.at[r, mine], s.far_send.at[r, k - 1], s.far_recv.at[r, mine], (target, self.t)
        )

    def from_outer(self, k):
        r, s = self.r, self.s
        other = lax.rem(self.b // RING + k, self.outer)
        return remote(
            s.far.at[r, other], s.far.at[r, other], s.far_send.at[r, k - 1], s.far_recv.at[r, other],
            (self.b ^ 1, self.t),
        )

    def back_batch(self, k, place):
        r, s = self.r, self.s
        return remote(
            s.full.at[r, self.t, place], s.full.at[r, self.t, place], s.three_send.at[r, k - 1],
            s.three_recv.at[r, place], (self.b ^ k, self.t),
        )

    def back_tensor(self, k, slot, place):
        r, s = self.r, self.s
        view = s.full.at[r, slot, place]
        return remote(view, view, s.four_send.at[r, k - 1, place], s.four_recv.at[r, slot, place], (self.b, self.t ^ k))

    def pass_piece(self, place):
        for k in (2, 3, 1):
            self.back_tensor(k, self.t, place).start()

    def step_one(self, half):
        group = COLUMNS // self.parts
        for slot in range(self.parts):
            at = slot * group + half * (group // 2)
            self.s.out[self.r, at : at + group // 2] = self.pack[at : at + group // 2].astype(BF16)
        for k in (2, 3, 1):
            self.across_tensor(half, k).start()

    def step_two(self):
        r, s = self.r, self.s
        group = COLUMNS // self.parts
        total = self.pack[pl.ds(self.t * group, group)]
        for k in range(1, self.parts):
            for half in range(2):
                self.from_tensor(half, k).wait_recv()
            total += s.one[r, self.t ^ k].astype(F32)
        total = total.reshape(RING, total.shape[0] * total.shape[1] // RING, 128)
        s.mid[r] = total
        s.mid_out[r] = total.astype(BF16)
        for k in range(1, RING):
            self.across_batch(k).start()

    def step_three(self):
        r, s = self.r, self.s
        total = s.mid[r, self.place]
        for k in range(1, RING):
            self.from_batch(k).wait_recv()
            total += s.two[r, self.place ^ k].astype(F32)
        if self.outer > 1:
            s.far[r, self.b // RING] = total.astype(BF16)
            for k in range(1, self.outer):
                self.across_outer(k).start()
            for k in range(1, self.outer):
                self.from_outer(k).wait_recv()
            total = s.far[r, 0].astype(F32)
            for other in range(1, self.outer):
                total += s.far[r, other].astype(F32)
            for k in range(1, self.outer):
                self.across_outer(k).wait_send()
        s.full[r, self.t, self.place] = total.astype(BF16)
        for k in range(1, RING):
            self.back_batch(k, self.place).start()
        self.pass_piece(self.place)

    def step_four(self):
        for k in range(1, RING):
            self.back_batch(k, self.place ^ k).wait_recv()
            self.pass_piece(self.place ^ k)

    def step_five(self):
        for k in range(1, self.parts):
            for place in range(RING):
                self.back_tensor(k, self.t ^ k, place).wait_recv()
        for k in range(1, self.parts):
            for half in range(2):
                self.across_tensor(half, k).wait_send()
            for place in range(RING):
                self.back_tensor(k, self.t, place).wait_send()
        for k in range(1, RING):
            self.across_batch(k).wait_send()
            self.back_batch(k, self.place).wait_send()


def finish_kernel(parts, frozen, state, grad, full, *refs):
    outs = Refs(**dict(zip(("frozen", "state", "grad", *OUTS), refs)))
    outs.frozen[...] = frozen[...]
    outs.state[...] = state[...].T[0:96]
    outs.grad[...] = grad[...].T[0:96]
    per = COLUMNS // parts
    for layer in range(LAYERS):

        def column(index):
            at = place_of(index)
            both = full[layer, at // per, 2 * (at % per) : 2 * (at % per) + 2]
            return both.astype(F32).reshape(96, 128)

        for k in range(6):
            outs.down[layer, :, 128 * k : 128 * k + 128] = column(k)
        for k in range(3):
            outs.expand[layer, :, 128 * k : 128 * k + 128] = column(6 + k)
            outs.reduce[layer, :, 128 * k : 128 * k + 128] = column(9 + k)
        outs.project[layer, :, 0:128] = column(12)
        outs.project[layer, :, 128:256] = column(13)
        last = column(14)
        outs.project[layer, :, 256:288] = last[:, 0:32]
        outs.mixing[layer] = pltpu.roll(last, 96, 1)[:, 0:96]
        small = column(15)
        outs.gate[layer : layer + 1, :] = small[0:1, 0:96]
        outs.gains[layer] = small[1:3, 0:96]


RAW = ("gate", "gains", "down", "project", "mixing", "expand", "reduce")
WEIGHTS = RAW[2:]
KEEP = ("lifted", "mixed", "query", "sums", "heads", "middle")


def keep_shapes(tokens):
    return (
        ((tokens, 128), F32),
        ((tokens, 128), F32),
        ((tokens, 128), BF16),
        ((16, tokens), F32),
        ((96, tokens), F32),
        ((tokens, 128), F32),
    )


def weight_scratch(model, units):
    return [
        pltpu.VMEM((128, model), BF16),
        pltpu.VMEM((128, 384), BF16),
        pltpu.VMEM((128, 128), BF16),
        pltpu.VMEM((128, units), BF16),
        pltpu.VMEM((128, units), BF16),
    ]


def tensor_barrier(b, t, parts):
    barrier = pltpu.get_barrier_semaphore()
    for k in range(1, parts):
        pl.semaphore_signal(barrier, inc=1, device_id=(b, t ^ k), device_id_type=MESH)
    return barrier


def vmem_specs(count):
    return [pl.BlockSpec(memory_space=pltpu.VMEM)] * count


OUTS = ("down", "gate", "gains", "project", "mixing", "expand", "reduce")
SUMS = (
    *("out", "one", "mid", "mid_out", "two", "far"),
    *("one_send", "one_recv", "two_send", "two_recv", "far_send", "far_recv"),
    *("three_send", "three_recv", "four_send", "four_recv"),
)
LOCAL = (
    *("k_s", "vt_s", "scores", "kv_send", "kv_recv", "do_s", "dot_s", "q_s", "qt_s", "v_s", "kt_s"),
    *("active", "slope"),
    *("terms", "terms_in", "dqkv", "terms_send", "terms_recv"),
)


def side_rest_kernel(parts, batch, *refs):
    refs = list(refs)

    def pop(count):
        taken, refs[:count] = refs[:count], []
        return taken

    second_f, side_in, cotangent, ids_ref = pop(4)
    raw = Refs(**dict(zip(RAW, pop(7))))
    state_one, *handed = pop(9)
    side_out, grad, full = pop(3)
    local = pop(8)
    first_f, kvt_zero = local[0:2]
    keep_zero = Refs(**dict(zip(KEEP, local[2:])))
    hand_sem = pop(1)[0]
    hand = [pltpu.make_async_copy(*pair, hand_sem.at[k]) for k, pair in enumerate(zip(handed, local))]
    for copy in hand:
        copy.start()
    kvt_one, prev, pack, raw.vectors = pop(4)
    keep_one = Refs(**dict(zip(KEEP, pop(6))))
    w_one = Refs(**dict(zip(WEIGHTS, pop(5))))
    w_zero = Refs(**dict(zip(WEIGHTS, pop(5))))
    c = Refs(**dict(zip(LOCAL, pop(len(LOCAL)))))
    s = Refs(**dict(zip(SUMS, pop(len(SUMS)))))
    s.full = full
    b = lax.axis_index("batch")
    t = lax.axis_index("tensor")
    barrier = tensor_barrier(b, t, parts)
    for k in range(1, RING):
        pl.semaphore_signal(barrier, inc=1, device_id=(b ^ k, t), device_id_type=MESH)
    outer = batch // RING
    for k in range(1, outer):
        other = lax.rem(b // RING + k, outer) * RING + lax.rem(b, RING)
        pl.semaphore_signal(barrier, inc=1, device_id=(other, t), device_id_type=MESH)
    load_vectors(raw.vectors, raw)
    load_side_weights(1, w_one, raw)
    load_side_weights(0, w_zero, raw)
    grad[...] = widened(cotangent)
    prev[...] = widened(side_in)
    pl.semaphore_wait(barrier, parts - 1 + RING - 1 + outer - 1)

    def prepare_lower():
        for copy in hand:
            copy.wait()
        side_prepare(0, parts, w_zero, raw, c, keep_zero, kvt_zero, ids_ref, True)

    first = Refs(
        kvt=kvt_one, k_s=c.k_s.at[1], vt_s=c.vt_s, scores=c.scores, kv_send=c.kv_send, kv_recv=c.kv_recv
    )
    side_forward(
        1, b, t, parts, second_f, state_one, w_one, raw, first, keep_one, ids_ref, side_out,
        lambda: None, prepare_lower, lambda index: None,
    )
    side_prepare(1, parts, w_one, raw, c, keep_one, kvt_one, ids_ref, False)
    upper = Sum(1, b, t, parts, batch, pack.at[1], s)
    lower = Sum(0, b, t, parts, batch, pack.at[0], s)
    side_backward(
        1, b, t, parts, second_f, state_one, w_one, raw, c, keep_one, grad, pack.at[1],
        lambda index: None, lambda: upper.step_one(0),
    )
    upper.step_one(1)

    def between(index):
        pl.when(index == 2)(upper.step_two)
        pl.when(index == 4)(upper.step_three)
        pl.when(index == 5)(upper.step_four)

    side_backward(
        0, b, t, parts, first_f, prev, w_zero, raw, c, keep_zero, grad, pack.at[0],
        between, lambda: lower.step_one(0),
    )
    lower.step_one(1)
    upper.step_five()
    lower.step_two()
    lower.step_three()
    lower.step_four()
    lower.step_five()


def side_rest_call(first_f, second_f, side_in, cotangent, ids_all, raw, state_one, kvt_zero, keep_zero, parts, batch):
    tokens, model = first_f.shape
    length = parts * tokens
    units = raw[5].shape[2]
    dma = pltpu.SemaphoreType.DMA
    vmem = pltpu.VMEM
    pairs = SIDE_HEADS // 2
    group = COLUMNS // parts
    piece = group * 96 // RING
    outs = (
        ((tokens, 128), F32),
        ((tokens, 128), F32),
        ((LAYERS, parts, RING, piece, 128), BF16),
    )
    outer = max(batch // RING, 1)
    return pl.pallas_call(
        functools.partial(side_rest_kernel, parts, batch),
        out_shape=tuple(jax.ShapeDtypeStruct(*o) for o in outs),
        in_specs=vmem_specs(12) + [pl.BlockSpec(memory_space=pl.ANY)] * 8,
        out_specs=tuple(vmem_specs(len(outs))),
        scratch_shapes=[
            vmem((tokens, model), BF16),
            vmem((parts, 192, tokens), BF16),
            *[vmem(*shape) for shape in keep_shapes(tokens)],
            dma((8,)),
            vmem((parts, 192, tokens), BF16),
            vmem((tokens, 128), F32),
            vmem((LAYERS, COLUMNS, 96, 128), F32),
            vmem((LAYERS, 8, 128), F32),
            *[vmem(*shape) for shape in keep_shapes(tokens)],
            *weight_scratch(model, units),
            *weight_scratch(model, units),
            vmem((LAYERS, length, 256), BF16),
            vmem((SIDE_HEADS, 16, length), BF16),
            vmem((2, length, tokens), F32),
            dma((3,)),
            dma((parts,)),
            vmem((tokens, 128), BF16),
            vmem((SIDE_HEADS, 16, tokens), BF16),
            vmem((LAYERS, tokens, 256), BF16),
            vmem((LAYERS, SIDE_HEADS, 16, tokens), BF16),
            vmem((LAYERS, length, 128), BF16),
            vmem((LAYERS, SIDE_HEADS, 16, length), BF16),
            vmem((LAYERS, tokens, units), BF16),
            vmem((LAYERS, tokens, units), F32),
            vmem((pairs, parts, 32, tokens), BF16),
            vmem((LAYERS, pairs, parts, 32, tokens), BF16),
            vmem((384, tokens), BF16),
            dma((LAYERS, pairs, parts - 1)),
            dma((LAYERS, pairs, parts)),
            vmem((LAYERS, COLUMNS, 96, 128), BF16),
            vmem((LAYERS, parts, group, 96, 128), BF16),
            vmem((LAYERS, RING, piece, 128), F32),
            vmem((LAYERS, RING, piece, 128), BF16),
            vmem((LAYERS, RING, piece, 128), BF16),
            vmem((LAYERS, outer, piece, 128), BF16),
            dma((LAYERS, 2, parts - 1)),
            dma((LAYERS, 2, parts)),
            dma((LAYERS, RING - 1)),
            dma((LAYERS, RING)),
            dma((LAYERS, max(outer - 1, 1))),
            dma((LAYERS, outer)),
            dma((LAYERS, RING - 1)),
            dma((LAYERS, RING)),
            dma((LAYERS, parts - 1, RING)),
            dma((LAYERS, parts, RING)),
        ],
        compiler_params=pltpu.CompilerParams(
            collective_id=5, has_side_effects=True, vmem_limit_bytes=62 << 20
        ),
    )(second_f, side_in, cotangent, ids_all, *raw, state_one, first_f, kvt_zero, *keep_zero)


def finish_call(frozen, state, grad, full, side, parts):
    tokens, model = frozen.shape
    units = 4 * side
    outs = (
        ((tokens, model), BF16),
        ((side, tokens), F32),
        ((side, tokens), F32),
        ((LAYERS, side, model), F32),
        ((LAYERS, side), F32),
        ((LAYERS, 2, side), F32),
        ((LAYERS, side, 3 * side), F32),
        ((LAYERS, side, side), F32),
        ((LAYERS, side, units), F32),
        ((LAYERS, side, units), F32),
    )
    frozen, state, grad, down, *others, reduce_grad = pl.pallas_call(
        functools.partial(finish_kernel, parts),
        out_shape=tuple(jax.ShapeDtypeStruct(*o) for o in outs),
        in_specs=vmem_specs(4),
        out_specs=tuple(vmem_specs(len(outs))),
        compiler_params=pltpu.CompilerParams(vmem_limit_bytes=62 << 20),
    )(frozen, state, grad, full)
    turn = (0, 2, 1)
    return (frozen, state.T, grad.T, down.transpose(turn), *others, reduce_grad.transpose(turn))


def per_device(
    hidden_rows,
    side_input,
    segment_ids,
    side_cotangent,
    backbone_gains,
    backbone_project,
    backbone_mixing,
    backbone_expand,
    backbone_reduce,
    side_down,
    side_gate,
    side_gains,
    side_project,
    side_mixing,
    side_expand,
    side_reduce,
):
    parts = lax.axis_size("tensor")
    batch = lax.axis_size("batch")
    side = side_input.shape[1]
    turn = (0, 2, 1)
    qkv = backbone_project.transpose(0, 2, 3, 1)
    raw = (
        side_gate,
        side_gains,
        side_down.transpose(turn),
        side_project,
        side_mixing,
        side_expand,
        side_reduce.transpose(turn),
    )
    side_turned, cotangent_turned = side_input.T, side_cotangent.T
    ids_row = segment_ids.reshape(1, -1)

    second_f, first_f, ids_all, state_one, kvt_zero, *keep_zero = front_call(
        hidden_rows,
        ids_row,
        backbone_gains,
        qkv,
        backbone_mixing,
        backbone_expand,
        backbone_reduce,
        side_turned,
        raw,
        parts,
    )
    state, grad, full = side_rest_call(
        first_f, second_f, side_turned, cotangent_turned, ids_all, raw, state_one, kvt_zero, keep_zero, parts, batch
    )
    return finish_call(second_f, state, grad, full, side, parts)


def solution(mesh):
    return jax.shard_map(
        per_device,
        mesh=mesh,
        in_specs=(
            P(("batch", "tensor"), None),
            P(("batch", "tensor"), None),
            P(("batch", "tensor")),
            P(("batch", "tensor"), None),
            P(),
            P(None, None, None, "tensor"),
            P(None, "tensor", None),
            P(None, None, "tensor"),
            P(None, "tensor", None),
            P(),
            P(),
            P(),
            P(),
            P(),
            P(),
            P(),
        ),
        out_specs=(
            P(("batch", "tensor"), None),
            P(("batch", "tensor"), None),
            P(("batch", "tensor"), None),
            P(),
            P(),
            P(),
            P(),
            P(),
            P(),
            P(),
        ),
        check_vma=False,
    )
```

profile of v0, /device:TPU:0, one launch (start us, length us, event | category | flops | bytes accessed | tf_op | source)
XLA Modules:
  0.0 233.9 jit_solution(2658637563559622035)
XLA Ops:
  0.6 115.2 %shard_map.231 = (bf16[512,768]{1,0:T(8,128)(2,1)}, bf16[512,768]{1,0:T(8,128)(2,1)}, s32[4,8,512]{2,1,0:T(8,128)}, f32[512,128]{1,0:T(8,128)}, bf16[4,192,512]{...) custom-call(bf16[512,768]{1,0:T(8,128)(2,1)} %refs_0_.1, ...), custom_call_target="tpu_custom_call" | custom-call | tf_op jit(solution)/shard_map/pallas_call | solution.py:525
  115.8 114.9 %shard_map.232 = (f32[512,128]{1,0:T(8,128)}, f32[512,128]{1,0:T(8,128)}, bf16[2,4,8,48,128]{4,3,2,1,0:T(8,128)(2,1)}) custom-call(bf16[512,768]{1,0:T(8,128)(2,1)} %get-tuple-element.34.refs_0_.frozen, bf16[96,512]{1,0:T(8,128)(2,1)} %bitcast.16, bf16[96,512]{1,0:T(8,128)(2,1)} %bitcast.17, s32[4,8,512]{2,1,0:T(8,128)} %get-tuple-element.35.refs_3_, ...), custom_call_target="tpu_custom_call" | custom-call | tf_op jit(solution)/shard_map/pallas_call | solution.py:1216
  230.7 3.2 %shard_map.233 = (bf16[512,768]{1,0:T(8,128)(2,1)}, f32[96,512]{1,0:T(8,128)}, f32[96,512]{1,0:T(8,128)}, f32[2,96,768]{2,1,0:T(8,128)}, f32[2,96]{1,0:T(2,128)}...) custom-call(bf16[512,768]{1,0:T(8,128)(2,1)} %get-tuple-element.34.r, ...), custom_call_target="tpu_custom_call" | custom-call | tf_op jit(solution)/shard_map/pallas_call | solution.py:1289
where the time goes:
time: 234 us
  Pallas kernels  233 us (100%)
    pallas_call x1, Pallas kernels, front_call(): pl.pallas_call(functools.partial(front_kernel, parts), out_shape=tuple((j...  115 us
    pallas_call x1, Pallas kernels, side_rest_call(): pl.pallas_call(functools.partial(side_rest_kernel, parts, batch), out_sha...  115 us

commit v1 on v0

--- a/solution.py
+++ b/solution.py
@@ -332,14 +332,26 @@
             c.acc[...] += nn(hidden, c.red_w[layer, self.t ^ index])
             return carry
 
-        lax.fori_loop(0, parts, feed, 0)
+        def far_up(index, carry):
+            hook(index)
+            c.spare[index - 2] = jax.nn.gelu(nn(c.normed[...], c.exp_w[layer, self.t ^ index])).astype(BF16)
+            return carry
+
+        def far_down(index, carry):
+            hook(index + 2)
+            c.acc[...] += nn(c.spare[index - 2], c.red_w[layer, self.t ^ index])
+            return carry
+
+        lax.fori_loop(0, 2, feed, 0)
+        lax.fori_loop(2, parts, far_up, 0)
+        lax.fori_loop(2, parts, far_down, 0)
 
 
 FRONT_SCRATCH = (
     *("vectors", "rows_all", "ids_scratch", "qkv_w", "mix_w", "exp_w", "red_w", "q_s", "k_s", "vt_s", "scores"),
     *("heads_buf", "acc", "normed", "load_sem", "qkv_sem", "row_send", "row_recv", "id_send", "id_recv"),
     *("head_send", "head_recv", "cross_send", "spread_send", "pass_send", "own_send", "w_recv", "pass_recv"),
-    *("own_recv", "side_k", "side_vt", "kv_send", "kv_recv"),
+    *("own_recv", "side_k", "side_vt", "kv_send", "kv_recv", "spare"),
 )
 
 
@@ -437,17 +449,21 @@
             def _():
                 for k in (1, 2):
                     weights.own(k, layer.sib).wait_recv()
-                if layer is lower:
-                    weights.start_forward(3)
-
-            @pl.when(index == 2)
+
+            @pl.when(index == 3)
+            def _():
+                for p in (1, 2):
+                    weights.wait_far(p)
+
+            @pl.when(index == 4)
             def _():
                 if layer is lower:
-                    weights.start_forward(4)
-
-            @pl.when(index == 3)
+                    for p in (3, 4):
+                        weights.start_forward(p)
+
+            @pl.when(index == 5)
             def _():
-                for p in range(1, 5):
+                for p in (3, 4):
                     weights.wait_far(p)
 
         return hook
@@ -565,6 +581,7 @@
             vmem((SIDE_HEADS, 16, length), BF16),
             dma((3,)),
             dma((parts,)),
+            vmem((2, tokens, model), BF16),
         ],
         compiler_params=pltpu.CompilerParams(
             collective_id=1, has_side_effects=True, vmem_limit_bytes=62 << 20

time: 234 us -> 248 us (1.060); the launches traced: 234 us -> 243 us
  Pallas kernels: 233 us -> 243 us
    pallas_call x1, Pallas kernels: 115 us -> 124 us  [side_rest_call(): pl.pallas_call(functools.partial(side_rest_kernel, parts, batch), out_sha...]
where the time goes in v1:
time: 248 us; the launch traced here: 243 us
  Pallas kernels  243 us (98%)
    pallas_call x1, Pallas kernels, side_rest_call(): pl.pallas_call(functools.partial(side_rest_kernel, parts, batch), out_sha...  124 us
    pallas_call x1, Pallas kernels, front_call(): pl.pallas_call(functools.partial(front_kernel, parts), out_shape=tuple((j...  115 us

profile of v1, /device:TPU:0, one launch (start us, length us, event | category | flops | bytes accessed | tf_op | source)
XLA Modules:
  0.0 243.4 jit_solution(11189744581794682274)
XLA Ops:
  0.6 115.0 %shard_map.231 = (bf16[512,768]{1,0:T(8,128)(2,1)}, bf16[512,768]{1,0:T(8,128)(2,1)}, s32[4,8,512]{2,1,0:T(8,128)}, f32[512,128]{1,0:T(8,128)}, bf16[4,192,512]{...) custom-call(bf16[512,768]{1,0:T(8,128)(2,1)} %refs_0_.1, ...), custom_call_target="tpu_custom_call" | custom-call | tf_op jit(solution)/shard_map/pallas_call | solution.py:541
  115.6 124.4 %shard_map.232 = (f32[512,128]{1,0:T(8,128)}, f32[512,128]{1,0:T(8,128)}, bf16[2,4,8,48,128]{4,3,2,1,0:T(8,128)(2,1)}) custom-call(bf16[512,768]{1,0:T(8,128)(2,1)} %get-tuple-element.34.refs_0_.frozen, bf16[96,512]{1,0:T(8,128)(2,1)} %bitcast.16, bf16[96,512]{1,0:T(8,128)(2,1)} %bitcast.17, s32[4,8,512]{2,1,0:T(8,128)} %get-tuple-element.35.refs_3_, ...), custom_call_target="tpu_custom_call" | custom-call | tf_op jit(solution)/shard_map/pallas_call | solution.py:1233
  240.0 3.2 %shard_map.233 = (bf16[512,768]{1,0:T(8,128)(2,1)}, f32[96,512]{1,0:T(8,128)}, f32[96,512]{1,0:T(8,128)}, f32[2,96,768]{2,1,0:T(8,128)}, f32[2,96]{1,0:T(2,128)}...) custom-call(bf16[512,768]{1,0:T(8,128)(2,1)} %get-tuple-element.34.r, ...), custom_call_target="tpu_custom_call" | custom-call | tf_op jit(solution)/shard_map/pallas_call | solution.py:1306
